TPU v7x, 32 devices: a whole 2x2x4 slice. The times are simulated.
32 devices in a mesh: gx: 16 (over z, y, core), gy: 2 (over x).
Axes of the slice: x: 2, y: 2, z: 4, core: 2. Of those that a mesh axis runs over, the one named last changes fastest.
Arguments:
- features: bfloat16 [16, 2, 3, 512, 192], P('gx', 'gy'), may hold values from -6 to 6
- weight: bfloat16 [5184, 192], replicated, may hold values from -0.078125 to 0.078125
- cotangent: bfloat16 [16, 2, 3, 64, 192], P('gx', 'gy'), may hold values from -6 to 6
- valid: int32 [16, 2, 3], P('gx', 'gy'), may hold values from 0 to 1, as said below
- local_rules: int32 [16, 2, 2, 12], P('gx', 'gy'), may hold values from 0 to 3, as said below
- local_codes: int32 [16, 2, 12], P('gx', 'gy'), may hold values from 0 to 7
- remote_rules: int32 [16, 2, 2, 3, 3], P('gx', 'gy'), may hold values from 0 to 3, as said below
- remote_codes: int32 [16, 2, 3, 3], P('gx', 'gy'), may hold values from 1 to 7, as said below
Outputs:
- output: bfloat16 [16, 2, 3, 64, 192], P('gx', 'gy')
- features_grad: bfloat16 [16, 2, 3, 512, 192], P('gx', 'gy')
- weight_grad: float32 [5184, 192], P('gx')
Inputs may be any that keep to these rules, and one draw needn't show every extreme that they name: `valid`: 1 marks a live brick slot; on each device the live slots come first and at least one slot is live. `local_rules`: entry [., ., 0, e] is a source slot and [., ., 1, e] a target slot of the same device; a target 3 marks an empty entry; non-empty entries name live slots. `remote_rules`: class m (third dimension) entry: a source slot on this device and a target slot on the device one step higher along gx (m = 0), along gy (m = 1) or along both (m = 2); a target 3 marks an empty entry; non-empty entries name live slots; devices at the upper end of an axis have no non-empty entries in the classes that cross it. `remote_codes`: the offset k mod 2 is 1 in classes 0 and 2, and the offset (k // 2) mod 2 is 1 in classes 1 and 2.
All inputs are finite; a program needn't handle non-finite values.
Results may differ from a plain program's by a relative error of at most 0.0045.
Values may be sent and summed in bfloat16 or wider, within the bound.
A program may use at most 128 MiB of HBM per device.

v0:
```python
from functools import partial

import jax
import jax.numpy as jnp
import numpy as np
from jax import lax
from jax.sharding import PartitionSpec as P


def shifted(block, axis, distance):
    devices = range(lax.axis_size(axis))
    route = [(i - distance, i) for i in devices if i - distance in devices]
    return lax.ppermute(block, axis, route)


def offset_table(row_x, row_y, row_z):
    code_list = np.arange(8)[:, None]
    step_x = code_list % 2
    step_y = code_list // 2 % 2
    step_z = code_list // 4
    inside = (
        ((step_x == 0) | (row_x[None, :] == 0))
        & ((step_y == 0) | (row_y[None, :] == 0))
        & ((step_z == 0) | (row_z[None, :] == 0))
    )
    source_row = (
        (row_x[None, :] + 4 * step_x) * 25
        + (row_y[None, :] + 4 * step_y) * 5
        + row_z[None, :]
        + 4 * step_z
    )
    return np.where(inside, source_row, 125).astype(np.int32)


def full_table():
    voxel_ids = np.arange(64)
    return offset_table(voxel_ids // 16, voxel_ids // 4 % 4, voxel_ids % 4)


def face_x_table():
    face_ids = np.arange(16)
    return offset_table(np.zeros(16, np.int64), face_ids // 4, face_ids % 4)


def face_y_table():
    face_ids = np.arange(16)
    return offset_table(face_ids // 4, np.zeros(16, np.int64), face_ids % 4)


def corner_table():
    edge_ids = np.arange(4)
    return offset_table(np.zeros(4, np.int64), np.zeros(4, np.int64), edge_ids)


def brick_patches(one_brick):
    channels = one_brick.shape[-1]
    cube = one_brick.reshape(8, 8, 8, channels)
    padded = jnp.pad(cube, ((1, 2), (1, 2), (1, 2), (0, 0)))
    tap_list = []
    for along_x in range(3):
        for along_y in range(3):
            for along_z in range(3):
                tap_list.append(
                    padded[
                        along_x : along_x + 9 : 2,
                        along_y : along_y + 9 : 2,
                        along_z : along_z + 9 : 2,
                        :,
                    ]
                )
    return jnp.stack(tap_list, axis=3).reshape(125, 27 * channels)


def fold_front(values):
    even_part = values[0:4, 1]
    odd_part = values[1:5, 0] + values[0:4, 2]
    stacked = jnp.stack([even_part, odd_part], axis=1)
    return stacked.reshape((8,) + stacked.shape[2:])


def brick_fold(patch_grads, channels):
    tap_grads = patch_grads.reshape(5, 5, 5, 3, 3, 3, channels)
    ordered = jnp.transpose(tap_grads, (0, 3, 1, 4, 2, 5, 6))
    along_x = fold_front(ordered)
    along_x = jnp.transpose(along_x, (1, 2, 0, 3, 4, 5))
    along_y = fold_front(along_x)
    along_y = jnp.transpose(along_y, (2, 3, 1, 0, 4))
    along_z = fold_front(along_y)
    return jnp.transpose(along_z, (1, 2, 0, 3)).reshape(512, channels)


def row_positions(sources, code_list, row_table):
    return sources[:, None] * 126 + jnp.asarray(row_table)[code_list]


def pick_float(index, table):
    flat_index = index.reshape(-1)
    hits = (flat_index[:, None] == jnp.arange(table.shape[0], dtype=jnp.int32)[None, :]).astype(
        jnp.float32
    )
    picked = jnp.dot(
        hits, table, precision=lax.Precision.HIGHEST, preferred_element_type=jnp.float32
    )
    return picked.reshape(index.shape + (table.shape[1],))


def pick_half(index, table):
    hits = (index[:, None] == jnp.arange(table.shape[0], dtype=jnp.int32)[None, :]).astype(
        jnp.bfloat16
    )
    flat_table = table.reshape(table.shape[0], -1)
    picked = jnp.dot(hits, flat_table, preferred_element_type=jnp.float32).astype(jnp.bfloat16)
    return picked.reshape((index.shape[0],) + table.shape[1:])


def collect(targets, pieces, bricks):
    hits = (targets[None, :] == jnp.arange(bricks, dtype=jnp.int32)[:, None]).astype(jnp.float32)
    flat_pieces = pieces.reshape(pieces.shape[0], -1)
    return jnp.dot(
        hits, flat_pieces, precision=lax.Precision.HIGHEST, preferred_element_type=jnp.float32
    )


def shards(
    features, weight, cotangent, valid, local_rules, local_codes, remote_rules, remote_codes
):
    bricks = features.shape[2]
    channels = features.shape[-1]
    live_slots = valid[0, 0]
    live_float = live_slots.astype(jnp.float32)[:, None, None]
    masked = features[0, 0] * live_slots.astype(jnp.bfloat16)[:, None, None]
    flat_patches = jax.vmap(brick_patches)(masked).reshape(bricks * 125, 27 * channels)
    partials = jnp.dot(flat_patches, weight, preferred_element_type=jnp.float32).reshape(
        bricks, 125, channels
    )
    zero_rows = jnp.zeros((bricks, 1, channels), jnp.float32)
    partial_rows = jnp.concatenate([partials, zero_rows], axis=1).reshape(bricks * 126, channels)
    index_x = row_positions(remote_rules[0, 0, 0, 0], remote_codes[0, 0, 0], face_x_table())
    index_y = row_positions(remote_rules[0, 0, 0, 1], remote_codes[0, 0, 1], face_y_table())
    index_xy = row_positions(remote_rules[0, 0, 0, 2], remote_codes[0, 0, 2], corner_table())
    index_local = row_positions(local_rules[0, 0, 0], local_codes[0, 0], full_table())
    target_x = remote_rules[0, 0, 1, 0]
    target_y = remote_rules[0, 0, 1, 1]
    target_xy = remote_rules[0, 0, 1, 2]
    target_local = local_rules[0, 0, 1]
    pieces_x = pick_float(index_x, partial_rows)
    pieces_y = pick_float(index_y, partial_rows)
    pieces_xy = pick_float(index_xy, partial_rows)
    got_x, got_x_target = (
        shifted(pieces_x.astype(jnp.bfloat16), "gx", 1).astype(pieces_x.dtype),
        shifted(target_x, "gx", 1),
    )
    got_y, got_y_target = (
        shifted(pieces_y.astype(jnp.bfloat16), "gy", 1).astype(pieces_y.dtype),
        shifted(target_y, "gy", 1),
    )
    middle_xy, middle_target = shifted((pieces_xy, target_xy), "gx", 1)
    got_xy, got_xy_target = shifted((middle_xy, middle_target), "gy", 1)
    local_pieces = pick_float(index_local, partial_rows)
    totals = collect(target_local, local_pieces, bricks).reshape(bricks, 4, 4, 4, channels)
    face_x_sum = collect(got_x_target, got_x, bricks).reshape(bricks, 1, 4, 4, channels)
    face_y_sum = collect(got_y_target, got_y, bricks).reshape(bricks, 4, 1, 4, channels)
    edge_sum = collect(got_xy_target, got_xy, bricks).reshape(bricks, 1, 1, 4, channels)
    totals = totals + jnp.pad(face_x_sum, ((0, 0), (0, 3), (0, 0), (0, 0), (0, 0)))
    totals = totals + jnp.pad(face_y_sum, ((0, 0), (0, 0), (0, 3), (0, 0), (0, 0)))
    totals = totals + jnp.pad(edge_sum, ((0, 0), (0, 3), (0, 3), (0, 0), (0, 0)))
    output = (totals.reshape(bricks, 64, channels) * live_float).astype(jnp.bfloat16)
    grad_out = cotangent[0, 0] * live_slots.astype(jnp.bfloat16)[:, None, None]
    grad_pad = jnp.concatenate([grad_out, jnp.zeros((1, 64, channels), jnp.bfloat16)], axis=0)
    grad_cube = grad_pad.reshape(bricks + 1, 4, 4, 4, channels)
    back_x = pick_half(got_x_target, grad_cube[:, 0].reshape(bricks + 1, 16, channels))
    back_y = pick_half(got_y_target, grad_cube[:, :, 0].reshape(bricks + 1, 16, channels))
    back_xy = pick_half(got_xy_target, grad_cube[:, 0, 0])
    return_x = shifted(back_x, "gx", -1)
    return_y = shifted(back_y, "gy", -1)
    middle_back = shifted(back_xy, "gy", -1)
    return_xy = shifted(middle_back, "gx", -1)
    index_all = jnp.concatenate(
        [index_local.reshape(-1), index_x.reshape(-1), index_y.reshape(-1), index_xy.reshape(-1)]
    )
    value_all = jnp.concatenate(
        [
            pick_half(target_local, grad_pad).reshape(-1, channels),
            return_x.reshape(-1, channels),
            return_y.reshape(-1, channels),
            return_xy.reshape(-1, channels),
        ],
        axis=0,
    )
    row_hits = (jnp.arange(bricks * 126, dtype=jnp.int32)[:, None] == index_all[None, :]).astype(
        jnp.bfloat16
    )
    grad_rows = jnp.dot(row_hits, value_all, preferred_element_type=jnp.float32)
    grad_rounded = grad_rows.reshape(bricks, 126, channels)[:, :125].astype(jnp.bfloat16)
    flat_grads = grad_rounded.reshape(bricks * 125, channels)
    patch_grads = lax.dot_general(
        flat_grads, weight, (((1,), (1,)), ((), ())), preferred_element_type=jnp.float32
    )
    weight_local = lax.dot_general(
        flat_patches, flat_grads, (((0,), (0,)), ((), ())), preferred_element_type=jnp.float32
    )
    folded = jax.vmap(partial(brick_fold, channels=channels))(
        patch_grads.reshape(bricks, 125, 27 * channels)
    )
    features_grad = (folded * live_float).astype(jnp.bfloat16)
    row_share = lax.psum_scatter(weight_local, "gx", scatter_dimension=0, tiled=True)
    weight_share = lax.psum(row_share, "gy")
    return (output[None, None], features_grad[None, None], weight_share)


def solution(mesh):
    return jax.shard_map(
        shards,
        mesh=mesh,
        in_specs=(
            P("gx", "gy", None, None, None),
            P(),
            P("gx", "gy", None, None, None),
            P("gx", "gy", None),
            P("gx", "gy", None, None),
            P("gx", "gy", None),
            P("gx", "gy", None, None, None),
            P("gx", "gy", None, None),
        ),
        out_specs=(P("gx", "gy", None, None, None), P("gx", "gy", None, None, None), P("gx", None)),
        check_vma=False,
    )
```

profile of v0, /device:TPU:0, one launch (start us, length us, event | category | flops | bytes accessed | tf_op | source)
XLA Modules:
  0.0 877.3 jit_solution(18175885702422755587)
XLA Ops:
  23.0 23.2 %slice.156 = bf16[3,5,5,5,192]{4,3,2,1,0:T(8,128)(2,1)} slice(bf16[3,11,11,11,192]{4,3,2,1,0:T(8,128)(2,1)S(1)} %pad.18), slice={[0:3:1], [0:9:2], [0:9:2], [0:9:2], [0:192:1]} | slice | bytes 288000 | tf_op jit(solution)/shard_map/vmap()/slice | solution.py:64
  46.1 23.0 %slice.157 = bf16[3,5,5,5,192]{4,3,2,1,0:T(8,128)(2,1)} slice(bf16[3,11,11,11,192]{4,3,2,1,0:T(8,128)(2,1)S(1)} %pad.18), slice={[0:3:1], [0:9:2], [0:9:2], [1:10:2], [0:192:1]} | slice | bytes 288000 | tf_op jit(solution)/shard_map/vmap()/slice | solution.py:64
  69.1 23.1 %slice.158 = bf16[3,5,5,5,192]{4,3,2,1,0:T(8,128)(2,1)} slice(bf16[3,11,11,11,192]{4,3,2,1,0:T(8,128)(2,1)S(1)} %pad.18), slice={[0:3:1], [0:9:2], [0:9:2], [2:11:2], [0:192:1]} | slice | bytes 288000 | tf_op jit(solution)/shard_map/vmap()/slice | solution.py:64
  92.2 23.0 %slice.159 = bf16[3,5,5,5,192]{4,3,2,1,0:T(8,128)(2,1)} slice(bf16[3,11,11,11,192]{4,3,2,1,0:T(8,128)(2,1)S(1)} %pad.18), slice={[0:3:1], [0:9:2], [1:10:2], [0:9:2], [0:192:1]} | slice | bytes 288000 | tf_op jit(solution)/shard_map/vmap()/slice | solution.py:64
  115.2 23.0 %slice.160 = bf16[3,5,5,5,192]{4,3,2,1,0:T(8,128)(2,1)} slice(bf16[3,11,11,11,192]{4,3,2,1,0:T(8,128)(2,1)S(1)} %pad.18), slice={[0:3:1], [0:9:2], [1:10:2], [1:10:2], [0:192:1]} | slice | bytes 288000 | tf_op jit(solution)/shard_map/vmap()/slice | solution.py:64
  138.2 23.0 %slice.161 = bf16[3,5,5,5,192]{4,3,2,1,0:T(8,128)(2,1)} slice(bf16[3,11,11,11,192]{4,3,2,1,0:T(8,128)(2,1)S(1)} %pad.18), slice={[0:3:1], [0:9:2], [1:10:2], [2:11:2], [0:192:1]} | slice | bytes 288000 | tf_op jit(solution)/shard_map/vmap()/slice | solution.py:64
  184.2 23.0 %slice.163 = bf16[3,5,5,5,192]{4,3,2,1,0:T(8,128)(2,1)} slice(bf16[3,11,11,11,192]{4,3,2,1,0:T(8,128)(2,1)S(1)} %pad.18), slice={[0:3:1], [0:9:2], [2:11:2], [1:10:2], [0:192:1]} | slice | bytes 288000 | tf_op jit(solution)/shard_map/vmap()/slice | solution.py:64
  230.2 23.0 %slice.165 = bf16[3,5,5,5,192]{4,3,2,1,0:T(8,128)(2,1)} slice(bf16[3,11,11,11,192]{4,3,2,1,0:T(8,128)(2,1)S(1)} %pad.18), slice={[0:3:1], [1:10:2], [0:9:2], [0:9:2], [0:192:1]} | slice | bytes 288000 | tf_op jit(solution)/shard_map/vmap()/slice | solution.py:64
  253.3 23.0 %slice.166 = bf16[3,5,5,5,192]{4,3,2,1,0:T(8,128)(2,1)} slice(bf16[3,11,11,11,192]{4,3,2,1,0:T(8,128)(2,1)S(1)} %pad.18), slice={[0:3:1], [1:10:2], [0:9:2], [1:10:2], [0:192:1]} | slice | bytes 288000 | tf_op jit(solution)/shard_map/vmap()/slice | solution.py:64
  276.3 23.0 %slice.167 = bf16[3,5,5,5,192]{4,3,2,1,0:T(8,128)(2,1)} slice(bf16[3,11,11,11,192]{4,3,2,1,0:T(8,128)(2,1)S(1)} %pad.18), slice={[0:3:1], [1:10:2], [0:9:2], [2:11:2], [0:192:1]} | slice | bytes 288000 | tf_op jit(solution)/shard_map/vmap()/slice | solution.py:64
  299.3 23.0 %slice.168 = bf16[3,5,5,5,192]{4,3,2,1,0:T(8,128)(2,1)} slice(bf16[3,11,11,11,192]{4,3,2,1,0:T(8,128)(2,1)S(1)} %pad.18), slice={[0:3:1], [1:10:2], [1:10:2], [0:9:2], [0:192:1]} | slice | bytes 288000 | tf_op jit(solution)/shard_map/vmap()/slice | solution.py:64
  322.3 23.0 %slice.169 = bf16[3,5,5,5,192]{4,3,2,1,0:T(8,128)(2,1)} slice(bf16[3,11,11,11,192]{4,3,2,1,0:T(8,128)(2,1)S(1)} %pad.18), slice={[0:3:1], [1:10:2], [1:10:2], [1:10:2], [0:192:1]} | slice | bytes 288000 | tf_op jit(solution)/shard_map/vmap()/slice | solution.py:64
  345.4 23.0 %slice.170 = bf16[3,5,5,5,192]{4,3,2,1,0:T(8,128)(2,1)} slice(bf16[3,11,11,11,192]{4,3,2,1,0:T(8,128)(2,1)S(1)} %pad.18), slice={[0:3:1], [1:10:2], [1:10:2], [2:11:2], [0:192:1]} | slice | bytes 288000 | tf_op jit(solution)/shard_map/vmap()/slice | solution.py:64
  368.4 23.0 %slice.171 = bf16[3,5,5,5,192]{4,3,2,1,0:T(8,128)(2,1)} slice(bf16[3,11,11,11,192]{4,3,2,1,0:T(8,128)(2,1)S(1)} %pad.18), slice={[0:3:1], [1:10:2], [2:11:2], [0:9:2], [0:192:1]} | slice | bytes 288000 | tf_op jit(solution)/shard_map/vmap()/slice | solution.py:64
  391.4 23.0 %slice.172 = bf16[3,5,5,5,192]{4,3,2,1,0:T(8,128)(2,1)} slice(bf16[3,11,11,11,192]{4,3,2,1,0:T(8,128)(2,1)S(1)} %pad.18), slice={[0:3:1], [1:10:2], [2:11:2], [1:10:2], [0:192:1]} | slice | bytes 288000 | tf_op jit(solution)/shard_map/vmap()/slice | solution.py:64
  414.4 23.0 %slice.173 = bf16[3,5,5,5,192]{4,3,2,1,0:T(8,128)(2,1)} slice(bf16[3,11,11,11,192]{4,3,2,1,0:T(8,128)(2,1)S(1)} %pad.18), slice={[0:3:1], [1:10:2], [2:11:2], [2:11:2], [0:192:1]} | slice | bytes 288000 | tf_op jit(solution)/shard_map/vmap()/slice | solution.py:64
  437.4 23.0 %slice.174 = bf16[3,5,5,5,192]{4,3,2,1,0:T(8,128)(2,1)} slice(bf16[3,11,11,11,192]{4,3,2,1,0:T(8,128)(2,1)S(1)} %pad.18), slice={[0:3:1], [2:11:2], [0:9:2], [0:9:2], [0:192:1]} | slice | bytes 288000 | tf_op jit(solution)/shard_map/vmap()/slice | solution.py:64
  460.5 23.0 %slice.175 = bf16[3,5,5,5,192]{4,3,2,1,0:T(8,128)(2,1)} slice(bf16[3,11,11,11,192]{4,3,2,1,0:T(8,128)(2,1)S(1)} %pad.18), slice={[0:3:1], [2:11:2], [0:9:2], [1:10:2], [0:192:1]} | slice | bytes 288000 | tf_op jit(solution)/shard_map/vmap()/slice | solution.py:64
  483.4 23.0 %slice.176 = bf16[3,5,5,5,192]{4,3,2,1,0:T(8,128)(2,1)} slice(bf16[3,11,11,11,192]{4,3,2,1,0:T(8,128)(2,1)S(1)} %pad.18), slice={[0:3:1], [2:11:2], [0:9:2], [2:11:2], [0:192:1]} | slice | bytes 288000 | tf_op jit(solution)/shard_map/vmap()/slice | solution.py:64
  506.5 23.0 %slice.177 = bf16[3,5,5,5,192]{4,3,2,1,0:T(8,128)(2,1)} slice(bf16[3,11,11,11,192]{4,3,2,1,0:T(8,128)(2,1)S(1)} %pad.18), slice={[0:3:1], [2:11:2], [1:10:2], [0:9:2], [0:192:1]} | slice | bytes 288000 | tf_op jit(solution)/shard_map/vmap()/slice | solution.py:64
  552.4 23.0 %slice.179 = bf16[3,5,5,5,192]{4,3,2,1,0:T(8,128)(2,1)} slice(bf16[3,11,11,11,192]{4,3,2,1,0:T(8,128)(2,1)S(1)} %pad.18), slice={[0:3:1], [2:11:2], [1:10:2], [2:11:2], [0:192:1]} | slice | bytes 288000 | tf_op jit(solution)/shard_map/vmap()/slice | solution.py:64
  575.5 23.0 %slice.180 = bf16[3,5,5,5,192]{4,3,2,1,0:T(8,128)(2,1)} slice(bf16[3,11,11,11,192]{4,3,2,1,0:T(8,128)(2,1)S(1)} %pad.18), slice={[0:3:1], [2:11:2], [2:11:2], [0:9:2], [0:192:1]} | slice | bytes 288000 | tf_op jit(solution)/shard_map/vmap()/slice | solution.py:64
  598.5 23.0 %slice.181 = bf16[3,5,5,5,192]{4,3,2,1,0:T(8,128)(2,1)} slice(bf16[3,11,11,11,192]{4,3,2,1,0:T(8,128)(2,1)S(1)} %pad.18), slice={[0:3:1], [2:11:2], [2:11:2], [1:10:2], [0:192:1]} | slice | bytes 288000 | tf_op jit(solution)/shard_map/vmap()/slice | solution.py:64
  770.1 73.5 %all-reduce.12.cloned.1.call-done = f32[5184,192]{0,1:T(8,128)} async-done(((f32[5184,192]{0,1:T(8,128)}), f32[5184,192]{0,1:T(8,128)}) %all-reduce.12.cloned.1.call-update) | async-done | bytes 3981328
  (198 shorter events, 258.6 us)
Async XLA Ops:
  7.2 836.4 %all-reduce.12.cloned.1.call-start = ((), (), s32[]{:S(2)}) async-start(), calls=%async_computation.1 | async-start | bytes 8060928
  8.6 692.5 %collective-permute-start = (s32[3]{0:T(128)}, s32[3]{0:T(128)}, u32[]{:S(2)}, u32[]{:S(2)}) collective-permute-start(s32[3]{0:T(128)} %get-tuple-element.15), channel_id=1, source_target_pairs={{0,2},{2,4},{4,6},{6,8},{8,10},{10,12},{12,14},{14,16},{16,18},{18... | collective-permute-start | bytes 44 | tf_op jit(solution)/shard_map/ppermute | solution.py:13
  11.4 692.5 %collective-permute-start.2 = (s32[3]{0:T(128)}, s32[3]{0:T(128)}, u32[]{:S(2)}, u32[]{:S(2)}) collective-permute-start(s32[3]{0:T(128)} %get-tuple-element.17), channel_id=1, source_target_pairs={{0,1},{2,3},{4,5},{6,7},{8,9},{10,11},{12,13},{14,15},{16,17},{18,... | collective-permute-start | bytes 44 | tf_op jit(solution)/shard_map/ppermute | solution.py:13
  16.2 679.0 %collective-permute-start.4 = (s32[3]{0:T(128)}, s32[3]{0:T(128)}, u32[]{:S(2)}, u32[]{:S(2)}) collective-permute-start(s32[3]{0:T(128)} %get-tuple-element.20), channel_id=1, source_target_pairs={{0,2},{2,4},{4,6},{6,8},{8,10},{10,12},{12,14},{14,16},{16,18},{18... | collective-permute-start | bytes 44 | tf_op jit(solution)/shard_map/ppermute | solution.py:13
  22.9 601.6 %copy-start.20 = (s32[1,1,3,3]{3,1,2,0:T(1,128)S(1)}, s32[1,1,3,3]{3,1,2,0:T(1,128)}, u32[]{:S(2)}) copy-start(s32[1,1,3,3]{3,1,2,0:T(1,128)} %param.19) | copy-start | bytes 112
  644.0 16.1 %copy-start.22 = (s32[1,1,12]{2,1,0:T(1,128)S(1)}, s32[1,1,12]{2,1,0:T(1,128)}, u32[]{:S(2)}) copy-start(s32[1,1,12]{2,1,0:T(1,128)} %param.17) | copy-start | bytes 148
  644.0 16.1 %copy-start.17 = (s32[8,16]{1,0:T(8,128)S(1)}, s32[8,16]{1,0:T(8,128)}, u32[]{:S(2)}) copy-start(s32[8,16]{1,0:T(8,128)} %constant.7.clone) | copy-start | bytes 1540
  644.0 21.3 %copy-start.15 = (bf16[1,1,3,64,192]{4,3,2,1,0:T(8,128)(2,1)S(1)}, bf16[1,1,3,64,192]{4,3,2,1,0:T(8,128)(2,1)}, u32[]{:S(2)}) copy-start(bf16[1,1,3,64,192]{4,3,2,1,0:T(8,128)(2,1)} %param.14) | copy-start | bytes 221188
  658.2 56.3 %collective-permute-start.3 = (bf16[3,16,192]{2,1,0:T(8,128)(2,1)S(1)}, bf16[3,16,192]{2,1,0:T(8,128)(2,1)}, u32[]{:S(2)}, u32[]{:S(2)}) collective-permute-start(bf16[3,16,192]{2,1,0:T(8,128)(2,1)S(1)} %convolution_convert_fusion.3), channel_id=1, source_target_pairs={{0,1},{2,3},{4,5},{6,7},{8,9},{10,11},{12,13},{14,15},{16,17},{18,... | collective-permute-start | bytes 55304 | tf_op jit(solution)/shard_map/ppermute | solution.py:13
  661.7 19.3 %copy-start.16 = (s32[8,4]{1,0:T(8,128)S(1)}, s32[8,4]{1,0:T(8,128)}, u32[]{:S(2)}) copy-start(s32[8,4]{1,0:T(8,128)} %constant.26.clone) | copy-start | bytes 388
  661.7 53.7 %collective-permute-start.1 = (bf16[3,16,192]{2,1,0:T(8,128)(2,1)}, bf16[3,16,192]{2,1,0:T(8,128)(2,1)}, u32[]{:S(2)}, u32[]{:S(2)}) collective-permute-start(bf16[3,16,192]{2,1,0:T(8,128)(2,1)} %convolution_convert_fusion.4), channel_id=1, source_target_pairs={{0,2},{2,4},{4,6},{6,8},{8,10},{10,12},{12,14},{14,16},{16,18},{18... | collective-permute-start | bytes 55304 | tf_op jit(solution)/shard_map/ppermute | solution.py:13
  665.4 19.2 %copy-start.13 = (s32[8,64]{1,0:T(8,128)S(1)}, s32[8,64]{1,0:T(8,128)}, u32[]{:S(2)}) copy-start(s32[8,64]{1,0:T(8,128)} %constant.27.clone) | copy-start | bytes 6148
  666.3 19.0 %slice-start = ((bf16[4,4,4,4,192]{4,3,2,1,0:T(4,128)(2,1)}), bf16[4,1,4,4,192]{4,3,2,1,0:T(4,128)(2,1)S(1)}, s32[]{:S(2)}) async-start(bf16[4,4,4,4,192]{4,3,2,1,0:T(4,128)(2,1)} %copy-done.14), calls=%async_computation.2 | async-start | bytes 65536 | tf_op jit(solution)/shard_map/slice | solution.py:171
  666.3 19.7 %slice-start.1 = ((bf16[4,4,4,4,192]{4,3,2,1,0:T(4,128)(2,1)}), bf16[4,4,1,4,192]{4,3,2,1,0:T(4,128)(2,1)S(1)}, s32[]{:S(2)}) async-start(bf16[4,4,4,4,192]{4,3,2,1,0:T(4,128)(2,1)} %copy-done.14), calls=%async_computation.3 | async-start | bytes 65536 | tf_op jit(solution)/shard_map/slice | solution.py:172
  695.1 2.6 collective-permute-start.5
  697.7 17.6 %copy-start.21 = (s32[3]{0:T(128)}, s32[3]{0:T(128)S(1)}, u32[]{:S(2)}) copy-start(s32[3]{0:T(128)S(1)} %collective-permute-done.5) | copy-start | bytes 40
  697.7 10.1 %collective-permute-start.6 = (f32[3,4,192]{2,1,0:T(4,128)}, f32[3,4,192]{2,1,0:T(4,128)}, u32[]{:S(2)}, u32[]{:S(2)}) collective-permute-start(f32[3,4,192]{2,1,0:T(4,128)} %fusion.28), channel_id=1, source_target_pairs={{0,2},{2,4},{4,6},{6,8},{8,10},{10,12},{12,14},{14,16},{16,18},{18... | collective-permute-start | bytes 27656 | tf_op jit(solution)/shard_map/ppermute | solution.py:13
  701.0 5.5 collective-permute-start.10
  704.0 17.8 %collective-permute-start.8 = (bf16[3,16,192]{2,1,0:T(8,128)(2,1)}, bf16[3,16,192]{2,1,0:T(8,128)(2,1)}, u32[]{:S(2)}, u32[]{:S(2)}) collective-permute-start(bf16[3,16,192]{2,1,0:T(8,128)(2,1)} %reshape.429), channel_id=1, source_target_pairs={{2,0},{4,2},{6,4},{8,6},{10,8},{12,10},{14,12},{16,14},{18,16},{20... | collective-permute-start | bytes 55304 | tf_op jit(solution)/shard_map/ppermute | solution.py:13
  706.5 6.7 collective-permute-start.11
  707.8 8.6 collective-permute-start.7
  713.2 8.5 collective-permute-start.9
  729.2 139.5 %all-reduce.10.cloned.1.call-start = ((), (), s32[]{:S(2)}) async-start(), calls=%async_computation | async-start | bytes 589824 | tf_op jit(solution)/shard_map/psum | solution.py:207
  767.5 77.9 %copy-start.19 = (f32[3]{0:T(128)S(1)}, f32[3]{0:T(128)}, u32[]{:S(2)}) copy-start(f32[3]{0:T(128)} %get-tuple-element.26) | copy-start | bytes 40
  (15 other events, 195.0 us)
Sparse Core Ops, SparseCore 0:
  729.3 114.2 all-reduce.11
  846.4 22.2 all-reduce.9
where the time goes:
time: 879 us; the launch traced here: 877 us
  local copies, waits for them, and re-layouts  687 us (78%)
  waiting for transfers between devices  98.2 us (11%)
  starting transfers between devices  28.9 us (3%)
  matrix products  27.1 us (3%)
  other arithmetic  20.9 us (2%)
  between operations  15.5 us (2%)
    slice x27, local copies, waits for them, and re-layouts, brick_patches(): padded[along_x:along_x + 9:2, along_y:along_y + 9:2, along_z:along_z + 9:...  602 us
    unnamed x3, waiting for transfers between devices  73.6 us
    ppermute x12, starting transfers between devices, shifted(): return lax.ppermute(block, axis, route)  28.6 us
    unnamed x79, local copies, waits for them, and re-layouts  26.2 us
    psum x1, waiting for transfers between devices, shards(): weight_share = lax.psum(row_share, 'gy')  22 us
  transfers between devices with their start and end apart: 14, of which 4 were waited for; matrix products, arithmetic and copies ran while one was open for 82% of the time, Pallas kernels for 0%

commit v1 on v0

v1 whole, which is shorter than its diff:
```python
import jax
import jax.numpy as jnp
import numpy as np
from jax import lax
from jax.experimental import pallas as pl
from jax.experimental.pallas import tpu as pltpu
from jax.sharding import PartitionSpec as P

BF = jnp.bfloat16
F32 = jnp.float32
MESH = pl.DeviceIdType.MESH

PAIRS = [(d, k) for d in range(8) for k in range(8) if k & ~d == 0]
PAIR_AT = {pair: at for at, pair in enumerate(PAIRS)}


def tap_list():
    taps = []
    for e in range(3):
        for f in range(3):
            for g in range(3):
                cls = (e != 1) + 2 * (f != 1) + 4 * (g != 1)
                shift = (e == 0) + 2 * (f == 0) + 4 * (g == 0)
                taps.append((9 * e + 3 * f + g, int(cls), int(shift)))
    return taps


TAPS = tap_list()


def bits(k):
    return k % 2, k // 2 % 2, k // 4


def rule_blocks(bricks):
    v = np.arange(64)
    coords = [v // 16, v // 4 % 4, v % 4]
    face = np.concatenate([v, (np.arange(16) // 4) * 16 + np.arange(16) % 4])
    blocks = []
    for d, k in PAIRS:
        hit = np.ones((64, 64), bool)
        for axis in range(3):
            row = coords[axis][:, None] + 4 * bits(k)[axis]
            col = coords[axis][None, :] + bits(d)[axis]
            hit &= row == col
        blocks.append(np.tile(hit[face], (1, bricks)))
    return np.stack(blocks).astype(np.float32)


def parity_order():
    rows = np.zeros(512, np.int64)
    for cls in range(8):
        px, py, pz = bits(cls)
        for v in range(64):
            a, b, c = v // 16, v // 4 % 4, v % 4
            rows[cls * 64 + v] = (2 * a + px) * 64 + (2 * b + py) * 8 + 2 * c + pz
    return rows


def face_picks(bricks):
    picks = np.zeros((3, bricks * 16, bricks * 64), np.float32)
    for t in range(bricks):
        for v in range(16):
            picks[0, t * 16 + v, t * 64 + v] = 1
            picks[1, t * 16 + v, t * 64 + (v // 4) * 16 + v % 4] = 1
            picks[2, t * 16 + v, t * 64 + v] = 1
    return picks.reshape(3 * bricks * 16, bricks * 64)


def chunks_of(rows, count):
    units = rows // 16
    cuts = [round(units * q / count) * 16 for q in range(count + 1)]
    return [(lo, hi - lo) for lo, hi in zip(cuts[:-1], cuts[1:])]


def dot(a, b):
    return jnp.dot(a, b, preferred_element_type=F32)


def dot_nt(a, b):
    return lax.dot_general(a, b, (((1,), (1,)), ((), ())), preferred_element_type=F32)


def dot_tn(a, b):
    return lax.dot_general(a, b, (((0,), (0,)), ((), ())), preferred_element_type=F32)


def make_kernel(ngx, ngy, bricks, local_count, remote_count, channels, chunk_count):
    rows = bricks * 64
    frows = bricks * 16
    share = 27 * channels // ngx
    padded = -(-share // 16) * 16
    chips = ngx // 2
    outer = ngx // 4
    chunks = chunks_of(padded, chunk_count)
    nq = len(chunks)
    ext = rows + 3 * frows

    def kernel(
        valid, lrules, lcodes, rrules, rcodes,
        feat, weight, cot, blocks, perm, perm_t, picks, picks_t, slot_of, eye,
        out, fgrad, wgrad,
        x_ref, xt_ref, m_ref, g_ref, t_ref, ge, gface, frecv, fsend, totals, fcls,
        wg, buf, recv_a, acc, recv_b, acc2, recv_c, final,
        s_g, r_g, s_f, r_f, s_a, r_a, s_b, r_b, s_c, r_c, s_d, r_d,
    ):
        i = lax.axis_index("gx")
        j = lax.axis_index("gy")
        core = lax.rem(i, 2)
        inner = lax.rem(i // 2, 2)
        z = i // 4
        up_i, dn_i = lax.rem(i + 1, ngx), lax.rem(i + ngx - 1, ngx)
        up_j, dn_j = lax.rem(j + 1, ngy), lax.rem(j + ngy - 1, ngy)
        ups = [(up_i, j), (i, up_j), (up_i, up_j)]
        downs = [(dn_i, j), (i, dn_j), (dn_i, dn_j)]
        core_peer = (i + 1 - 2 * core, j)
        inner_peer = (i + 2 - 4 * inner, j)
        outer_peers = [(lax.rem(i + 4 * k, ngx), j) for k in range(1, outer)]
        gy_peers = [(i, lax.rem(j + k, ngy)) for k in range(1, ngy)]
        peers = ups + downs + [core_peer, inner_peer] + outer_peers + gy_peers

        barrier = pltpu.get_barrier_semaphore()
        for peer in peers:
            pl.semaphore_signal(barrier, inc=1, device_id=peer, device_id_type=MESH)

        live = [valid[0, 0, s] for s in range(bricks)]
        live_f = [v.astype(F32) for v in live]
        for s in range(bricks):
            ge[s * 64 : (s + 1) * 64] = (cot[0, 0, s].astype(F32) * live_f[s]).astype(BF)
        own = ge[0:rows]
        gface[...] = dot(picks[0 : 2 * frows], own).astype(BF)
        pl.semaphore_wait(barrier, len(peers))

        def remote(src, dst, ssem, rsem, peer):
            return pltpu.make_async_remote_copy(
                src_ref=src, dst_ref=dst, send_sem=ssem, recv_sem=rsem,
                device_id=peer, device_id_type=MESH,
            )

        face_copies = []
        for c in range(3):
            src = gface.at[pl.ds(frows * (c % 2), frows)]
            dst = ge.at[pl.ds(rows + c * frows, frows)]
            copy = remote(src, dst, s_g.at[c], r_g.at[c], downs[c])
            copy.start()
            face_copies.append(copy)

        for s in range(bricks):
            moved = dot(perm[...], feat[0, 0, s]) * live_f[s]
            for cls in range(8):
                x_ref[cls, s * 64 : (s + 1) * 64] = moved[cls * 64 : (cls + 1) * 64].astype(BF)
        for cls in range(8):
            xt_ref[cls] = dot_nt(eye[...], x_ref[cls]).astype(BF)

        groups = 8 * bricks
        row_id = lax.broadcasted_iota(jnp.int32, (4 * groups, 128), 0)
        lane_id = lax.broadcasted_iota(jnp.int32, (4 * groups, 128), 1)
        counts = jnp.zeros((4 * groups, 128), F32)

        def count(total, kind, source, target, code):
            at = jnp.where(target < bricks, kind * groups + 8 * target + code, -1)
            return total + jnp.where((row_id == at) & (lane_id == source), 1.0, 0.0)

        for e in range(local_count):
            counts = count(counts, 0, lrules[0, 0, 0, e], lrules[0, 0, 1, e], lcodes[0, 0, e])
        for c in range(3):
            for e in range(remote_count):
                counts = count(
                    counts, c + 1, rrules[0, 0, 0, c, e], rrules[0, 0, 1, c, e], rcodes[0, 0, c, e]
                )
        spread = dot(counts.astype(BF), slot_of[...])

        for d in range(8):
            codes = [k for k in range(8) if k & ~d == 0]
            full = {k: blocks[PAIR_AT[(d, k)]].astype(F32) for k in codes}
            for kind in range(4):
                need = (0, 1, 2, 3)[kind]
                lo, hi = ((0, 64), (0, 16), (64, 80), (0, 16))[kind]
                for t in range(bricks):
                    total = jnp.zeros((hi - lo, rows), F32)
                    for k in codes:
                        if k & need == need:
                            at = kind * groups + 8 * t + k
                            total = total + spread[at : at + 1] * full[k][lo:hi]
                    first = t * 64 if kind == 0 else rows + (kind - 1) * frows + t * 16
                    m_ref[d, first : first + hi - lo] = total.astype(BF)

        for copy in face_copies:
            copy.wait()
        grads = ge[...]
        for d in range(8):
            g_ref[d] = dot_tn(m_ref[d], grads).astype(BF)

        a_copies = []
        built = 0
        for tap, cls, shift in TAPS:
            wg[tap * channels : (tap + 1) * channels] = dot(xt_ref[cls], g_ref[shift])
            while built < chips and 2 * share * (built + 1) <= (tap + 1) * channels:
                for h in range(2):
                    first = share * (2 * built + h)
                    block = wg[first : first + share].astype(BF)
                    if padded > share:
                        fill = jnp.zeros((padded - share, channels), BF)
                        block = jnp.concatenate([block, fill], axis=0)
                    buf[2 * built + h] = block
                copy = remote(
                    buf.at[2 * built + 1 - core], recv_a.at[built],
                    s_a.at[built], r_a.at[built], core_peer,
                )
                copy.start()
                a_copies.append(copy)
                built += 1

        for d in range(8):
            total = None
            for tap, cls, shift in TAPS:
                if shift == d:
                    term = dot(x_ref[cls], weight[tap * channels : (tap + 1) * channels])
                    total = term if total is None else total + term
            t_ref[d] = total

        for copy in a_copies:
            copy.wait_recv()
        b_copies = []
        for q, (lo, n) in enumerate(chunks):
            for m in range(chips):
                mine = buf[2 * m + core, lo : lo + n].astype(F32)
                acc[m % 2, m // 2, lo : lo + n] = (
                    mine + recv_a[m, lo : lo + n].astype(F32)
                ).astype(BF)
            copy = remote(
                acc.at[1 - inner, :, pl.ds(lo, n)], recv_b.at[:, pl.ds(lo, n)],
                s_b.at[q], r_b.at[q], inner_peer,
            )
            copy.start()
            b_copies.append(copy)

        total = None
        for d in range(8):
            value = t_ref[d]
            high = value.astype(BF)
            low = (value - high.astype(F32)).astype(BF)
            term = dot(m_ref[d], high) + dot(m_ref[d], low)
            total = term if total is None else total + term
        totals[...] = total[0:rows]
        fsend[...] = total[rows:ext].astype(BF)
        f_copies = []
        for c in range(3):
            span = pl.ds(c * frows, frows)
            copy = remote(fsend.at[span], frecv.at[span], s_f.at[c], r_f.at[c], ups[c])
            copy.start()
            f_copies.append(copy)

        def second(q):
            lo, n = chunks[q]
            b_copies[q].wait_recv()
            for o in range(outer):
                acc2[o, lo : lo + n] = (
                    acc[inner, o, lo : lo + n].astype(F32) + recv_b[o, lo : lo + n].astype(F32)
                ).astype(BF)
            started = []
            for k in range(1, outer):
                copy = remote(
                    acc2.at[lax.rem(z + k, outer), pl.ds(lo, n)], recv_c.at[k - 1, pl.ds(lo, n)],
                    s_c.at[q, k - 1], r_c.at[q, k - 1], outer_peers[k - 1],
                )
                copy.start()
                started.append(copy)
            return started

        def third(q):
            lo, n = chunks[q]
            total = acc2[z, lo : lo + n].astype(F32)
            for k in range(1, outer):
                c_copies[q][k - 1].wait_recv()
                total = total + recv_c[k - 1, lo : lo + n].astype(F32)
            final[j, lo : lo + n] = total.astype(BF)
            started = []
            for k in range(1, ngy):
                mine = final.at[j, pl.ds(lo, n)]
                copy = remote(mine, mine, s_d.at[q, k - 1], r_d.at[q, k - 1], gy_peers[k - 1])
                copy.start()
                started.append(copy)
            return started

        def feature_class(cls):
            total = None
            for tap, tap_cls, shift in TAPS:
                if tap_cls == cls:
                    term = dot_nt(g_ref[shift], weight[tap * channels : (tap + 1) * channels])
                    total = term if total is None else total + term
            for s in range(bricks):
                fcls[s, cls * 64 : (cls + 1) * 64] = (
                    total[s * 64 : (s + 1) * 64] * live_f[s]
                ).astype(BF)

        c_copies = []
        for cls in range(4):
            feature_class(cls)
        c_copies.append(second(0))
        for cls in range(4, 7):
            feature_class(cls)
        for q in range(1, nq):
            c_copies.append(second(q))
            if q == 1:
                feature_class(7)
        for s in range(bricks):
            fgrad[0, 0, s] = dot(perm_t[...], fcls[s]).astype(BF)

        for copy in f_copies:
            copy.wait()
        result = totals[...] + dot(picks_t[...], frecv[...])
        for s in range(bricks):
            out[0, 0, s] = (result[s * 64 : (s + 1) * 64] * live_f[s]).astype(BF)

        d_copies = [third(q) for q in range(nq)]
        for q, (lo, n) in enumerate(chunks):
            for copy in d_copies[q]:
                copy.wait_recv()
            total = final[0, lo : lo + n].astype(F32)
            for k in range(1, ngy):
                total = total + final[k, lo : lo + n].astype(F32)
            keep = min(n, share - lo)
            wgrad[lo : lo + keep] = total[0:keep]

        for copy in a_copies + b_copies:
            copy.wait_send()
        for copies in c_copies + d_copies:
            for copy in copies:
                copy.wait_send()

    dma = pltpu.SemaphoreType.DMA
    scratch = [
        pltpu.VMEM((8, rows, channels), BF),
        pltpu.VMEM((8, channels, rows), BF),
        pltpu.VMEM((8, ext, rows), BF),
        pltpu.VMEM((8, rows, channels), BF),
        pltpu.VMEM((8, rows, channels), F32),
        pltpu.VMEM((ext, channels), BF),
        pltpu.VMEM((2 * frows, channels), BF),
        pltpu.VMEM((3 * frows, channels), BF),
        pltpu.VMEM((3 * frows, channels), BF),
        pltpu.VMEM((rows, channels), F32),
        pltpu.VMEM((bricks, 512, channels), BF),
        pltpu.VMEM((27 * channels, channels), F32),
        pltpu.VMEM((ngx, padded, channels), BF),
        pltpu.VMEM((chips, padded, channels), BF),
        pltpu.VMEM((2, outer, padded, channels), BF),
        pltpu.VMEM((outer, padded, channels), BF),
        pltpu.VMEM((outer, padded, channels), BF),
        pltpu.VMEM((outer - 1, padded, channels), BF),
        pltpu.VMEM((ngy, padded, channels), BF),
        dma((3,)), dma((3,)), dma((3,)), dma((3,)),
        dma((chips,)), dma((chips,)), dma((nq,)), dma((nq,)),
        dma((nq, outer - 1)), dma((nq, outer - 1)),
        dma((nq, ngy - 1)), dma((nq, ngy - 1)),
    ]
    return kernel, scratch, share


def solution(mesh):
    ngx, ngy = mesh.shape["gx"], mesh.shape["gy"]

    def shards(
        features, weight, cotangent, valid, local_rules, local_codes, remote_rules, remote_codes
    ):
        bricks = features.shape[2]
        channels = features.shape[-1]
        local_count = local_codes.shape[-1]
        remote_count = remote_codes.shape[-1]
        kernel, scratch, share = make_kernel(
            ngx, ngy, bricks, local_count, remote_count, channels, 3
        )
        order = parity_order()
        perm = np.zeros((512, 512), np.float32)
        perm[np.arange(512), order] = 1
        picks = face_picks(bricks)
        slot_of = (np.arange(128)[:, None] == (np.arange(bricks * 64) // 64)[None, :]).astype(
            np.float32
        )
        consts = [
            jnp.asarray(c, BF)
            for c in (
                rule_blocks(bricks), perm, perm.T, picks, picks.T, slot_of,
                np.eye(channels, dtype=np.float32),
            )
        ]
        vmem = pl.BlockSpec(memory_space=pltpu.VMEM)
        smem = pl.BlockSpec(memory_space=pltpu.SMEM)
        return pl.pallas_call(
            kernel,
            out_shape=(
                jax.ShapeDtypeStruct(cotangent.shape, BF),
                jax.ShapeDtypeStruct(features.shape, BF),
                jax.ShapeDtypeStruct((share, channels), F32),
            ),
            in_specs=[smem] * 5 + [vmem] * 10,
            out_specs=(vmem, vmem, vmem),
            scratch_shapes=scratch,
            compiler_params=pltpu.CompilerParams(
                collective_id=0, has_side_effects=True, vmem_limit_bytes=56 * 1024 * 1024
            ),
        )(
            valid, local_rules, local_codes, remote_rules, remote_codes,
            features, weight, cotangent, *consts,
        )

    return jax.shard_map(
        shards,
        mesh=mesh,
        in_specs=(
            P("gx", "gy", None, None, None),
            P(),
            P("gx", "gy", None, None, None),
            P("gx", "gy", None),
            P("gx", "gy", None, None),
            P("gx", "gy", None),
            P("gx", "gy", None, None, None),
            P("gx", "gy", None, None),
        ),
        out_specs=(P("gx", "gy", None, None, None), P("gx", "gy", None, None, None), P("gx", None)),
        check_vma=False,
    )
```

time: 879 us -> 59.2 us (0.07)
  local copies, waits for them, and re-layouts: 687 us -> 13.8 us
  waiting for transfers between devices: 98.2 us -> 0 us
  Pallas kernels: 0 us -> 44.4 us
  starting transfers between devices: 28.9 us -> 0 us
  matrix products: 27.1 us -> 0 us
  other arithmetic: 20.9 us -> 0 us
  between operations: 15.5 us -> 0.65 us
    slice x33 -> x0, local copies, waits for them, and re-layouts: 602 us -> none  [the longest x27 602 us: brick_patches(): padded[along_x:along_x + 9:2, along_y:along_y + 9:2, along_z:along_z + 9:...]
    unnamed x3 -> x0, waiting for transfers between devices: 73.6 us -> none
    pallas_call x0 -> x1, Pallas kernels: none -> 44.4 us  [shards(): pl.pallas_call(kernel, out_shape=(jax.ShapeDtypeStruct(cotangent.shape, B...]
    ppermute x12 -> x0, starting transfers between devices: 28.6 us -> none  [shifted(): return lax.ppermute(block, axis, route)]
    dot_general x16 -> x0, matrix products: 27.1 us -> none  [the longest x1 7.37 us: shards(): lax.dot_general(flat_grads, weight, (((1,), (1,)), ((), ())), preferred_e...]
    reshape x16 -> x0, local copies, waits for them, and re-layouts: 24.6 us -> none  [the longest x1 9.92 us: shards(): jax.vmap(brick_patches)(masked).reshape(bricks * 125, 27 * channels)]
    psum x1 -> x0, waiting for transfers between devices: 22 us -> none  [shards(): weight_share = lax.psum(row_share, 'gy')]
    another operation x11 -> x0, local copies, waits for them, and re-layouts: 17.4 us -> none  [the longest x1 8.94 us: fold_front(): stacked = jnp.stack([even_part, odd_part], axis=1)]
  transfers between devices with their start and end apart: 14 -> 0, of which waited for: 4 -> 0; matrix products, arithmetic and copies ran while one was open for 82% -> 0% of each run, Pallas kernels for 0% -> 0%
where the time goes in v1:
time: 59.2 us; the launch traced here: 58.8 us
  Pallas kernels  44.4 us (75%)
  local copies, waits for them, and re-layouts  13.8 us (23%)
  between operations  0.65 us (1%)
    pallas_call x1, Pallas kernels, shards(): pl.pallas_call(kernel, out_shape=(jax.ShapeDtypeStruct(cotangent.shape, B...  44.4 us
    unnamed x7, local copies, waits for them, and re-layouts  9.68 us
    pallas_call x2, local copies, waits for them, and re-layouts, shards(): pl.pallas_call(kernel, out_shape=(jax.ShapeDtypeStruct(cotangent.shape, B...  4.09 us

profile of v1, /device:TPU:0, one launch (start us, length us, event | category | flops | bytes accessed | tf_op | source)
XLA Modules:
  0.0 58.8 jit_solution(11326638996572283912)
XLA Ops:
  0.6 1.3 %copy.19.rcodes = s32[1,1,3,3]{3,2,1,0:T(4,128)} copy(s32[1,1,3,3]{3,1,2,0:T(1,128)} %param.22) | data formatting | bytes 72 | tf_op args[7]
  1.9 1.3 %copy.18.rrules = s32[1,1,2,3,3]{4,3,2,1,0:T(4,128)} copy(s32[1,1,2,3,3]{4,2,3,1,0:T(2,128)} %param.21) | data formatting | bytes 144 | tf_op args[6]
  3.2 2.2 %copy.20.feat = bf16[1,1,3,512,192]{4,3,2,1,0:T(8,128)(2,1)} copy(bf16[1,1,3,512,192]{3,4,2,1,0:T(8,128)(2,1)} %param.15) | data formatting | bytes 1179648 | tf_op args[0]
  5.4 4.3 %copy.21.weight = bf16[5184,192]{1,0:T(8,128)(2,1)} copy(bf16[5184,192]{0,1:T(8,128)(2,1)} %param.16) | data formatting | bytes 3981312 | tf_op args[1]
  9.7 44.4 %shard_map.166 = (bf16[1,1,3,64,192]{4,3,2,1,0:T(8,128)(2,1)}, bf16[1,1,3,512,192]{4,3,2,1,0:T(8,128)(2,1)}, f32[324,192]{1,0:T(8,128)}) custom-call(s32[1,1,3]{2,1,0:T(1,128)} %valid.1, s32[1,1,2,12]{3,2,1,0:T(2,128)} %lrules.1, s32[1,1,12]{2,1,0:T(1,128)} %lcodes.1, s32[1,1,2,3,3]{4,3,2,1,0:T(4,128)} %copy.18.rrules, s32[1,1,3,3]{3,2,1,0:T(4,128)} %copy.19.rcodes, ...), custom_call_target="tpu_custom_call" | custom-call | tf_op jit(solution)/shard_map/pallas_call | solution.py:390
  54.1 0.0 copy-start
  54.1 1.9 %copy.23 = f32[324,192]{0,1:T(8,128)} copy(f32[324,192]{1,0:T(8,128)} %get-tuple-element.5) | data formatting | bytes 497664 | tf_op jit(solution)/shard_map/pallas_call | solution.py:390
  56.0 2.2 %copy.22 = bf16[1,1,3,512,192]{3,4,2,1,0:T(8,128)(2,1)} copy(bf16[1,1,3,512,192]{4,3,2,1,0:T(8,128)(2,1)} %get-tuple-element.4) | data formatting | bytes 1179648 | tf_op jit(solution)/shard_map/pallas_call | solution.py:390
  58.2 0.0 copy-done
  58.2 0.6 %copy.25 = bf16[1,1,3,64,192]{4,3,2,1,0:T(8,128)(2,1)} copy(bf16[1,1,3,64,192]{4,3,2,1,0:T(8,128)(2,1)S(1)} %copy-done) | data formatting | bytes 147456
Async XLA Ops:
  54.1 4.1 %copy-start = (bf16[1,1,3,64,192]{4,3,2,1,0:T(8,128)(2,1)S(1)}, bf16[1,1,3,64,192]{4,3,2,1,0:T(8,128)(2,1)}, u32[]{:S(2)}) copy-start(bf16[1,1,3,64,192]{4,3,2,1,0:T(8,128)(2,1)} %get-tuple-element.9) | copy-start | bytes 221188

commit v2 on v1

--- a/solution.py
+++ b/solution.py
@@ -89,7 +89,11 @@
     rows = bricks * 64
     frows = bricks * 16
     share = 27 * channels // ngx
-    padded = -(-share // 16) * 16
+    half = 128
+    left = -(-share // 16) * 16
+    right = -(-share // 32) * 16
+    padded = left + right
+    wide = 2 * half
     chips = ngx // 2
     outer = ngx // 4
     chunks = chunks_of(padded, chunk_count)
@@ -98,10 +102,10 @@
 
     def kernel(
         valid, lrules, lcodes, rrules, rcodes,
-        feat, weight, cot, blocks, perm, perm_t, picks, picks_t, slot_of, eye,
+        feat, weight, cot, blocks, perm, picks, picks_t, slot_of, eye, twice,
         out, fgrad, wgrad,
-        x_ref, xt_ref, m_ref, g_ref, t_ref, ge, gface, frecv, fsend, totals, fcls,
-        wg, buf, recv_a, acc, recv_b, acc2, recv_c, final,
+        w_ref, x_ref, xt_ref, m_ref, g_ref, t_ref, ge, gface, frecv, fsend, totals, fcls,
+        wg, buf, recv_a, acc, recv_b, acc2, recv_c, final, summed,
         s_g, r_g, s_f, r_f, s_a, r_a, s_b, r_b, s_c, r_c, s_d, r_d,
     ):
         i = lax.axis_index("gx")
@@ -128,6 +132,8 @@
         for s in range(bricks):
             ge[s * 64 : (s + 1) * 64] = (cot[0, 0, s].astype(F32) * live_f[s]).astype(BF)
         own = ge[0:rows]
+        for tap in range(27):
+            w_ref[tap] = weight[:, tap * channels : (tap + 1) * channels]
         gface[...] = dot(picks[0 : 2 * frows], own).astype(BF)
         pl.semaphore_wait(barrier, len(peers))
 
@@ -146,7 +152,7 @@
             face_copies.append(copy)
 
         for s in range(bricks):
-            moved = dot(perm[...], feat[0, 0, s]) * live_f[s]
+            moved = dot_nt(perm[...], feat[0, 0, s]) * live_f[s]
             for cls in range(8):
                 x_ref[cls, s * 64 : (s + 1) * 64] = moved[cls * 64 : (cls + 1) * 64].astype(BF)
         for cls in range(8):
@@ -166,7 +172,7 @@
         for c in range(3):
             for e in range(remote_count):
                 counts = count(
-                    counts, c + 1, rrules[0, 0, 0, c, e], rrules[0, 0, 1, c, e], rcodes[0, 0, c, e]
+                    counts, c + 1, rrules[0, 0, c, 0, e], rrules[0, 0, c, 1, e], rcodes[0, c, 0, e]
                 )
         spread = dot(counts.astype(BF), slot_of[...])
 
@@ -187,22 +193,26 @@
 
         for copy in face_copies:
             copy.wait()
-        grads = ge[...]
+        grads = dot(ge[...], twice[...]).astype(BF)
         for d in range(8):
             g_ref[d] = dot_tn(m_ref[d], grads).astype(BF)
 
         a_copies = []
         built = 0
+        first_lanes = lax.broadcasted_iota(jnp.int32, (right, half), 1) < channels - half
         for tap, cls, shift in TAPS:
             wg[tap * channels : (tap + 1) * channels] = dot(xt_ref[cls], g_ref[shift])
             while built < chips and 2 * share * (built + 1) <= (tap + 1) * channels:
                 for h in range(2):
                     first = share * (2 * built + h)
-                    block = wg[first : first + share].astype(BF)
-                    if padded > share:
-                        fill = jnp.zeros((padded - share, channels), BF)
-                        block = jnp.concatenate([block, fill], axis=0)
-                    buf[2 * built + h] = block
+                    block = wg[first : first + share, 0:half].astype(BF)
+                    tail = wg[first : first + share, half:wide]
+                    fill = jnp.zeros((left - share, half), BF)
+                    buf[2 * built + h, 0:left] = jnp.concatenate([block, fill], axis=0)
+                    rest = jnp.zeros((2 * right - share, half), F32)
+                    later = jnp.concatenate([tail[right:share], rest], axis=0)
+                    packed = jnp.where(first_lanes, tail[0:right], later)
+                    buf[2 * built + h, left:padded] = packed.astype(BF)
                 copy = remote(
                     buf.at[2 * built + 1 - core], recv_a.at[built],
                     s_a.at[built], r_a.at[built], core_peer,
@@ -215,7 +225,7 @@
             total = None
             for tap, cls, shift in TAPS:
                 if shift == d:
-                    term = dot(x_ref[cls], weight[tap * channels : (tap + 1) * channels])
+                    term = dot_nt(x_ref[cls], w_ref[tap])
                     total = term if total is None else total + term
             t_ref[d] = total
 
@@ -287,7 +297,7 @@
             total = None
             for tap, tap_cls, shift in TAPS:
                 if tap_cls == cls:
-                    term = dot_nt(g_ref[shift], weight[tap * channels : (tap + 1) * channels])
+                    term = dot(g_ref[shift, :, 0:channels], w_ref[tap])
                     total = term if total is None else total + term
             for s in range(bricks):
                 fcls[s, cls * 64 : (cls + 1) * 64] = (
@@ -305,7 +315,7 @@
             if q == 1:
                 feature_class(7)
         for s in range(bricks):
-            fgrad[0, 0, s] = dot(perm_t[...], fcls[s]).astype(BF)
+            fgrad[0, 0, s] = dot_tn(fcls[s], perm[...]).astype(BF)
 
         for copy in f_copies:
             copy.wait()
@@ -320,8 +330,12 @@
             total = final[0, lo : lo + n].astype(F32)
             for k in range(1, ngy):
                 total = total + final[k, lo : lo + n].astype(F32)
-            keep = min(n, share - lo)
-            wgrad[lo : lo + keep] = total[0:keep]
+            summed[lo : lo + n] = total
+        wgrad[0:half] = jnp.transpose(summed[0:left])[:, 0:share]
+        turned = jnp.transpose(summed[left:padded])
+        tail = channels - half
+        wgrad[half:channels, 0:right] = turned[0:tail]
+        wgrad[half:channels, right:share] = turned[tail : 2 * tail, 0 : share - right]
 
         for copy in a_copies + b_copies:
             copy.wait_send()
@@ -331,10 +345,11 @@
 
     dma = pltpu.SemaphoreType.DMA
     scratch = [
+        pltpu.VMEM((27, channels, channels), BF),
         pltpu.VMEM((8, rows, channels), BF),
         pltpu.VMEM((8, channels, rows), BF),
         pltpu.VMEM((8, ext, rows), BF),
-        pltpu.VMEM((8, rows, channels), BF),
+        pltpu.VMEM((8, rows, wide), BF),
         pltpu.VMEM((8, rows, channels), F32),
         pltpu.VMEM((ext, channels), BF),
         pltpu.VMEM((2 * frows, channels), BF),
@@ -342,14 +357,15 @@
         pltpu.VMEM((3 * frows, channels), BF),
         pltpu.VMEM((rows, channels), F32),
         pltpu.VMEM((bricks, 512, channels), BF),
-        pltpu.VMEM((27 * channels, channels), F32),
-        pltpu.VMEM((ngx, padded, channels), BF),
-        pltpu.VMEM((chips, padded, channels), BF),
-        pltpu.VMEM((2, outer, padded, channels), BF),
-        pltpu.VMEM((outer, padded, channels), BF),
-        pltpu.VMEM((outer, padded, channels), BF),
-        pltpu.VMEM((outer - 1, padded, channels), BF),
-        pltpu.VMEM((ngy, padded, channels), BF),
+        pltpu.VMEM((27 * channels, wide), F32),
+        pltpu.VMEM((ngx, padded, half), BF),
+        pltpu.VMEM((chips, padded, half), BF),
+        pltpu.VMEM((2, outer, padded, half), BF),
+        pltpu.VMEM((outer, padded, half), BF),
+        pltpu.VMEM((outer, padded, half), BF),
+        pltpu.VMEM((outer - 1, padded, half), BF),
+        pltpu.VMEM((ngy, padded, half), BF),
+        pltpu.VMEM((padded, half), F32),
         dma((3,)), dma((3,)), dma((3,)), dma((3,)),
         dma((chips,)), dma((chips,)), dma((nq,)), dma((nq,)),
         dma((nq, outer - 1)), dma((nq, outer - 1)),
@@ -369,7 +385,7 @@
         local_count = local_codes.shape[-1]
         remote_count = remote_codes.shape[-1]
         kernel, scratch, share = make_kernel(
-            ngx, ngy, bricks, local_count, remote_count, channels, 3
+            ngx, ngy, bricks, local_count, remote_count, channels, 4
         )
         order = parity_order()
         perm = np.zeros((512, 512), np.float32)
@@ -378,21 +394,24 @@
         slot_of = (np.arange(128)[:, None] == (np.arange(bricks * 64) // 64)[None, :]).astype(
             np.float32
         )
+        twice = np.zeros((channels, 256), np.float32)
+        twice[np.arange(channels), np.arange(channels)] = 1
+        twice[np.arange(128, channels), np.arange(128, channels) + channels - 128] = 1
         consts = [
             jnp.asarray(c, BF)
             for c in (
-                rule_blocks(bricks), perm, perm.T, picks, picks.T, slot_of,
-                np.eye(channels, dtype=np.float32),
+                rule_blocks(bricks), perm, picks, picks.T, slot_of,
+                np.eye(channels, dtype=np.float32), twice,
             )
         ]
         vmem = pl.BlockSpec(memory_space=pltpu.VMEM)
         smem = pl.BlockSpec(memory_space=pltpu.SMEM)
-        return pl.pallas_call(
+        out, fgrad, wgrad = pl.pallas_call(
             kernel,
             out_shape=(
                 jax.ShapeDtypeStruct(cotangent.shape, BF),
-                jax.ShapeDtypeStruct(features.shape, BF),
-                jax.ShapeDtypeStruct((share, channels), F32),
+                jax.ShapeDtypeStruct((1, 1, bricks, channels, 512), BF),
+                jax.ShapeDtypeStruct((channels, share), F32),
             ),
             in_specs=[smem] * 5 + [vmem] * 10,
             out_specs=(vmem, vmem, vmem),
@@ -401,9 +420,11 @@
                 collective_id=0, has_side_effects=True, vmem_limit_bytes=56 * 1024 * 1024
             ),
         )(
-            valid, local_rules, local_codes, remote_rules, remote_codes,
-            features, weight, cotangent, *consts,
+            valid, local_rules, local_codes, jnp.swapaxes(remote_rules, 2, 3),
+            jnp.swapaxes(remote_codes, 1, 2), jnp.swapaxes(features, 3, 4), weight.T,
+            cotangent, *consts,
         )
+        return out, jnp.swapaxes(fgrad, 3, 4), wgrad.T
 
     return jax.shard_map(
         shards,

time: 59.2 us -> 45.3 us (0.77)
  local copies, waits for them, and re-layouts: 13.8 us -> 5.15 us
  Pallas kernels: 44.4 us -> 39.3 us
    pallas_call x1, Pallas kernels: 44.4 us -> 39.3 us  [shards(): pl.pallas_call(kernel, out_shape=(jax.ShapeDtypeStruct(cotangent.shape, B...]
    unnamed x7 -> x3, local copies, waits for them, and re-layouts: 9.68 us -> 5.15 us
    pallas_call x2 -> x0, local copies, waits for them, and re-layouts: 4.09 us -> none  [shards(): pl.pallas_call(kernel, out_shape=(jax.ShapeDtypeStruct(cotangent.shape, B...]
where the time goes in v2:
time: 45.3 us; the launch traced here: 45.1 us
  Pallas kernels  39.3 us (87%)
  local copies, waits for them, and re-layouts  5.15 us (11%)
  between operations  0.64 us (1%)
    pallas_call x1, Pallas kernels, shards(): pl.pallas_call(kernel, out_shape=(jax.ShapeDtypeStruct(cotangent.shape, B...  39.3 us
    unnamed x3, local copies, waits for them, and re-layouts  5.15 us

profile of v2, /device:TPU:0, one launch (start us, length us, event | category | flops | bytes accessed | tf_op | source)
XLA Modules:
  0.0 45.1 jit_solution(2267048029938273756)
XLA Ops:
  0.6 39.3 %shard_map.166 = (bf16[1,1,3,64,192]{4,3,2,1,0:T(8,128)(2,1)}, bf16[1,1,3,192,512]{4,3,2,1,0:T(8,128)(2,1)}, f32[192,324]{1,0:T(8,128)}) custom-call(s32[1,1,3]{2,1,0:T(1,128)} %valid.1, s32[1,1,2,12]{3,2,1,0:T(2,128)} %lrules.1, s32[1,1,12]{2,1,0:T(1,128)} %lcodes.1, s32[1,1,3,2,3]{4,3,2,1,0:T(2,128)} %bitcast.10, s32[1,3,1,3]{3,2,1,0:T(1,128)} %bitcast.11, ...), custom_call_target="tpu_custom_call" | custom-call | tf_op jit(solution)/shard_map/pallas_call | solution.py:409
  40.0 1.5 %copy.21 = bf16[1,1,3,64,192]{4,3,2,1,0:T(8,128)(2,1)} copy(bf16[1,1,3,64,192]{4,3,2,1,0:T(8,128)(2,1)} %get-tuple-element.12) | data formatting | bytes 147456
  41.5 1.9 %copy.22 = bf16[1,1,3,512,192]{3,4,2,1,0:T(8,128)(2,1)} copy(bf16[1,1,3,512,192]{3,4,2,1,0:T(8,128)(2,1)} %bitcast.7) | data formatting | bytes 1179648
  43.4 1.7 %copy.23 = f32[324,192]{0,1:T(8,128)} copy(f32[324,192]{0,1:T(8,128)} %bitcast.9) | data formatting | bytes 497664

commit v3 on v2

--- a/solution.py
+++ b/solution.py
@@ -96,17 +96,23 @@
     wide = 2 * half
     chips = ngx // 2
     outer = ngx // 4
-    chunks = chunks_of(padded, chunk_count)
+    part = 16 * max(1, padded // (32 * ngy))
+    base = padded - part * ngy
+    chunks = chunks_of(base, min(chunk_count, base // 16))
     nq = len(chunks)
+    parts = chunks_of(part, min(chunk_count, part // 16))
+    np_ = len(parts)
     ext = rows + 3 * frows
 
     def kernel(
         valid, lrules, lcodes, rrules, rcodes,
-        feat, weight, cot, blocks, perm, picks, picks_t, slot_of, eye, twice,
+        feat, weight_hbm, cot, blocks, perm, picks, picks_t, slot_of, eye, twice,
         out, fgrad, wgrad,
-        w_ref, x_ref, xt_ref, m_ref, g_ref, t_ref, ge, gface, frecv, fsend, totals, fcls,
+        weight, w_ref, x_ref, xt_ref, m_ref, g_ref, t_ref, ge, gface, frecv, fsend, totals, fcls,
         wg, buf, recv_a, acc, recv_b, acc2, recv_c, final, summed,
+        xacc, recv_x, yacc, recv_y, zacc, recv_z, gathered,
         s_g, r_g, s_f, r_f, s_a, r_a, s_b, r_b, s_c, r_c, s_d, r_d,
+        s_x, r_x, s_y, r_y, s_z, r_z, s_w, r_w, s_fetch,
     ):
         i = lax.axis_index("gx")
         j = lax.axis_index("gy")
@@ -123,6 +129,8 @@
         gy_peers = [(i, lax.rem(j + k, ngy)) for k in range(1, ngy)]
         peers = ups + downs + [core_peer, inner_peer] + outer_peers + gy_peers
 
+        fetch = pltpu.make_async_copy(weight_hbm, weight, s_fetch)
+        fetch.start()
         barrier = pltpu.get_barrier_semaphore()
         for peer in peers:
             pl.semaphore_signal(barrier, inc=1, device_id=peer, device_id_type=MESH)
@@ -132,8 +140,6 @@
         for s in range(bricks):
             ge[s * 64 : (s + 1) * 64] = (cot[0, 0, s].astype(F32) * live_f[s]).astype(BF)
         own = ge[0:rows]
-        for tap in range(27):
-            w_ref[tap] = weight[:, tap * channels : (tap + 1) * channels]
         gface[...] = dot(picks[0 : 2 * frows], own).astype(BF)
         pl.semaphore_wait(barrier, len(peers))
 
@@ -221,7 +227,11 @@
                 a_copies.append(copy)
                 built += 1
 
-        for d in range(8):
+        fetch.wait()
+        for tap in range(27):
+            w_ref[tap] = weight[:, tap * channels : (tap + 1) * channels]
+
+        def forward(d):
             total = None
             for tap, cls, shift in TAPS:
                 if shift == d:
@@ -231,19 +241,41 @@
 
         for copy in a_copies:
             copy.wait_recv()
-        b_copies = []
-        for q, (lo, n) in enumerate(chunks):
-            for m in range(chips):
-                mine = buf[2 * m + core, lo : lo + n].astype(F32)
-                acc[m % 2, m // 2, lo : lo + n] = (
-                    mine + recv_a[m, lo : lo + n].astype(F32)
-                ).astype(BF)
-            copy = remote(
-                acc.at[1 - inner, :, pl.ds(lo, n)], recv_b.at[:, pl.ds(lo, n)],
-                s_b.at[q], r_b.at[q], inner_peer,
-            )
-            copy.start()
-            b_copies.append(copy)
+
+        def core_sum(m, lo, n):
+            mine = buf[2 * m + core, lo : lo + n].astype(F32)
+            return (mine + recv_a[m, lo : lo + n].astype(F32)).astype(BF)
+
+        x_copies, b_copies = [], []
+        for q in range(max(nq, np_)):
+            if q < np_:
+                lo, n = parts[q]
+                for m in range(chips):
+                    for g in range(ngy):
+                        xacc[g, m % 2, m // 2, lo : lo + n] = core_sum(m, base + g * part + lo, n)
+                started = []
+                for k in range(1, ngy):
+                    copy = remote(
+                        xacc.at[lax.rem(j + k, ngy), :, :, pl.ds(lo, n)],
+                        recv_x.at[k - 1, :, :, pl.ds(lo, n)],
+                        s_x.at[q, k - 1], r_x.at[q, k - 1], gy_peers[k - 1],
+                    )
+                    copy.start()
+                    started.append(copy)
+                x_copies.append(started)
+            if q < nq:
+                lo, n = chunks[q]
+                for m in range(chips):
+                    acc[m % 2, m // 2, lo : lo + n] = core_sum(m, lo, n)
+                copy = remote(
+                    acc.at[1 - inner, :, pl.ds(lo, n)], recv_b.at[:, pl.ds(lo, n)],
+                    s_b.at[q], r_b.at[q], inner_peer,
+                )
+                copy.start()
+                b_copies.append(copy)
+
+        for d in range(8):
+            forward(d)
 
         total = None
         for d in range(8):
@@ -293,6 +325,55 @@
                 started.append(copy)
             return started
 
+        def part_x(q):
+            lo, n = parts[q]
+            for copy in x_copies[q]:
+                copy.wait_recv()
+            for h in range(2):
+                for o in range(outer):
+                    total = xacc[j, h, o, lo : lo + n].astype(F32)
+                    for k in range(1, ngy):
+                        total = total + recv_x[k - 1, h, o, lo : lo + n].astype(F32)
+                    yacc[h, o, lo : lo + n] = total.astype(BF)
+            copy = remote(
+                yacc.at[1 - inner, :, pl.ds(lo, n)], recv_y.at[:, pl.ds(lo, n)],
+                s_y.at[q], r_y.at[q], inner_peer,
+            )
+            copy.start()
+            return copy
+
+        def part_y(q):
+            lo, n = parts[q]
+            y_copies[q].wait_recv()
+            for o in range(outer):
+                zacc[o, lo : lo + n] = (
+                    yacc[inner, o, lo : lo + n].astype(F32) + recv_y[o, lo : lo + n].astype(F32)
+                ).astype(BF)
+            started = []
+            for k in range(1, outer):
+                copy = remote(
+                    zacc.at[lax.rem(z + k, outer), pl.ds(lo, n)], recv_z.at[k - 1, pl.ds(lo, n)],
+                    s_z.at[q, k - 1], r_z.at[q, k - 1], outer_peers[k - 1],
+                )
+                copy.start()
+                started.append(copy)
+            return started
+
+        def part_z(q):
+            lo, n = parts[q]
+            total = zacc[z, lo : lo + n].astype(F32)
+            for k in range(1, outer):
+                z_copies[q][k - 1].wait_recv()
+                total = total + recv_z[k - 1, lo : lo + n].astype(F32)
+            gathered[j, lo : lo + n] = total
+            started = []
+            for k in range(1, ngy):
+                mine = gathered.at[j, pl.ds(lo, n)]
+                copy = remote(mine, mine, s_w.at[q, k - 1], r_w.at[q, k - 1], gy_peers[k - 1])
+                copy.start()
+                started.append(copy)
+            return started
+
         def feature_class(cls):
             total = None
             for tap, tap_cls, shift in TAPS:
@@ -304,26 +385,34 @@
                     total[s * 64 : (s + 1) * 64] * live_f[s]
                 ).astype(BF)
 
-        c_copies = []
-        for cls in range(4):
+        c_copies, d_copies, y_copies, z_copies, w_copies = [], [], [], [], []
+        feature_class(0)
+        feature_class(1)
+        for q in range(max(nq, np_)):
+            if q < nq:
+                c_copies.append(second(q))
+            if q < np_:
+                y_copies.append(part_x(q))
+            for cls in (2, 3, 4) if q == 0 else (5, 6) if q == 1 else ():
+                feature_class(cls)
+        for cls in range(5, 8) if max(nq, np_) == 1 else (7,):
             feature_class(cls)
-        c_copies.append(second(0))
-        for cls in range(4, 7):
-            feature_class(cls)
-        for q in range(1, nq):
-            c_copies.append(second(q))
-            if q == 1:
-                feature_class(7)
-        for s in range(bricks):
-            fgrad[0, 0, s] = dot_tn(fcls[s], perm[...]).astype(BF)
-
+        for q in range(max(nq, np_)):
+            if q < np_:
+                z_copies.append(part_y(q))
+            if q == 0:
+                for s in range(bricks):
+                    fgrad[0, 0, s] = dot_tn(fcls[s], perm[...]).astype(BF)
+            if q < nq:
+                d_copies.append(third(q))
         for copy in f_copies:
             copy.wait()
         result = totals[...] + dot(picks_t[...], frecv[...])
         for s in range(bricks):
             out[0, 0, s] = (result[s * 64 : (s + 1) * 64] * live_f[s]).astype(BF)
-
-        d_copies = [third(q) for q in range(nq)]
+        for q in range(np_):
+            w_copies.append(part_z(q))
+
         for q, (lo, n) in enumerate(chunks):
             for copy in d_copies[q]:
                 copy.wait_recv()
@@ -331,20 +420,26 @@
             for k in range(1, ngy):
                 total = total + final[k, lo : lo + n].astype(F32)
             summed[lo : lo + n] = total
+        for copies in w_copies:
+            for copy in copies:
+                copy.wait_recv()
+        for g in range(ngy):
+            summed[base + g * part : base + (g + 1) * part] = gathered[g]
         wgrad[0:half] = jnp.transpose(summed[0:left])[:, 0:share]
         turned = jnp.transpose(summed[left:padded])
         tail = channels - half
         wgrad[half:channels, 0:right] = turned[0:tail]
         wgrad[half:channels, right:share] = turned[tail : 2 * tail, 0 : share - right]
 
-        for copy in a_copies + b_copies:
+        for copy in a_copies + b_copies + y_copies:
             copy.wait_send()
-        for copies in c_copies + d_copies:
+        for copies in c_copies + d_copies + x_copies + z_copies + w_copies:
             for copy in copies:
                 copy.wait_send()
 
     dma = pltpu.SemaphoreType.DMA
     scratch = [
+        pltpu.VMEM((channels, 27 * channels), BF),
         pltpu.VMEM((27, channels, channels), BF),
         pltpu.VMEM((8, rows, channels), BF),
         pltpu.VMEM((8, channels, rows), BF),
@@ -360,18 +455,37 @@
         pltpu.VMEM((27 * channels, wide), F32),
         pltpu.VMEM((ngx, padded, half), BF),
         pltpu.VMEM((chips, padded, half), BF),
-        pltpu.VMEM((2, outer, padded, half), BF),
-        pltpu.VMEM((outer, padded, half), BF),
-        pltpu.VMEM((outer, padded, half), BF),
-        pltpu.VMEM((outer - 1, padded, half), BF),
-        pltpu.VMEM((ngy, padded, half), BF),
+        pltpu.VMEM((2, outer, base, half), BF),
+        pltpu.VMEM((outer, base, half), BF),
+        pltpu.VMEM((outer, base, half), BF),
+        pltpu.VMEM((outer - 1, base, half), BF),
+        pltpu.VMEM((ngy, base, half), BF),
         pltpu.VMEM((padded, half), F32),
+        pltpu.VMEM((ngy, 2, outer, part, half), BF),
+        pltpu.VMEM((ngy - 1, 2, outer, part, half), BF),
+        pltpu.VMEM((2, outer, part, half), BF),
+        pltpu.VMEM((outer, part, half), BF),
+        pltpu.VMEM((outer, part, half), BF),
+        pltpu.VMEM((outer - 1, part, half), BF),
+        pltpu.VMEM((ngy, part, half), F32),
         dma((3,)), dma((3,)), dma((3,)), dma((3,)),
         dma((chips,)), dma((chips,)), dma((nq,)), dma((nq,)),
         dma((nq, outer - 1)), dma((nq, outer - 1)),
         dma((nq, ngy - 1)), dma((nq, ngy - 1)),
+        dma((np_, ngy - 1)), dma((np_, ngy - 1)), dma((np_,)), dma((np_,)),
+        dma((np_, outer - 1)), dma((np_, outer - 1)), dma((np_, ngy - 1)), dma((np_, ngy - 1)),
+        dma,
     ]
     return kernel, scratch, share
+
+
+def hand_over(a, b, c, a_out, b_out, c_out, sems):
+    pairs = ((a, a_out), (b, b_out), (c, c_out))
+    copies = [pltpu.make_async_copy(src, dst, sems.at[at]) for at, (src, dst) in enumerate(pairs)]
+    for copy in copies:
+        copy.start()
+    for copy in copies:
+        copy.wait()
 
 
 def solution(mesh):
@@ -385,7 +499,7 @@
         local_count = local_codes.shape[-1]
         remote_count = remote_codes.shape[-1]
         kernel, scratch, share = make_kernel(
-            ngx, ngy, bricks, local_count, remote_count, channels, 4
+            ngx, ngy, bricks, local_count, remote_count, channels, 2
         )
         order = parity_order()
         perm = np.zeros((512, 512), np.float32)
@@ -405,6 +519,8 @@
             )
         ]
         vmem = pl.BlockSpec(memory_space=pltpu.VMEM)
+        anywhere = pl.BlockSpec(memory_space=pl.ANY)
+        hbm = pl.BlockSpec(memory_space=pltpu.HBM)
         smem = pl.BlockSpec(memory_space=pltpu.SMEM)
         out, fgrad, wgrad = pl.pallas_call(
             kernel,
@@ -413,7 +529,7 @@
                 jax.ShapeDtypeStruct((1, 1, bricks, channels, 512), BF),
                 jax.ShapeDtypeStruct((channels, share), F32),
             ),
-            in_specs=[smem] * 5 + [vmem] * 10,
+            in_specs=[smem] * 5 + [vmem, anywhere] + [vmem] * 8,
             out_specs=(vmem, vmem, vmem),
             scratch_shapes=scratch,
             compiler_params=pltpu.CompilerParams(
@@ -424,6 +540,13 @@
             jnp.swapaxes(remote_codes, 1, 2), jnp.swapaxes(features, 3, 4), weight.T,
             cotangent, *consts,
         )
+        out, fgrad, wgrad = pl.pallas_call(
+            hand_over,
+            out_shape=tuple(jax.ShapeDtypeStruct(a.shape, a.dtype) for a in (out, fgrad, wgrad)),
+            in_specs=[hbm] * 3,
+            out_specs=(hbm,) * 3,
+            scratch_shapes=[pltpu.SemaphoreType.DMA((3,))],
+        )(out, fgrad, wgrad)
         return out, jnp.swapaxes(fgrad, 3, 4), wgrad.T
 
     return jax.shard_map(

time: 45.3 us -> 67.5 us (1.49)
  Pallas kernels: 39.3 us -> 66.8 us
  local copies, waits for them, and re-layouts: 5.15 us -> 0 us
    pallas_call x0 -> x1, Pallas kernels: none -> 30.9 us  [shards(): pl.pallas_call(hand_over, out_shape=tuple((jax.ShapeDtypeStruct(a.shape,...]
    unnamed x3 -> x0, local copies, waits for them, and re-layouts: 5.15 us -> none
    pallas_call x1, Pallas kernels: 39.3 us -> 35.8 us  [shards(): pl.pallas_call(kernel, out_shape=(jax.ShapeDtypeStruct(cotangent.shape, B...]
where the time goes in v3:
time: 67.5 us; the launch traced here: 67.4 us
  Pallas kernels  66.8 us (99%)
    pallas_call x1, Pallas kernels, shards(): pl.pallas_call(kernel, out_shape=(jax.ShapeDtypeStruct(cotangent.shape, B...  35.8 us
    pallas_call x1, Pallas kernels, shards(): pl.pallas_call(hand_over, out_shape=tuple((jax.ShapeDtypeStruct(a.shape,...  30.9 us

profile of v3, /device:TPU:0, one launch (start us, length us, event | category | flops | bytes accessed | tf_op | source)
XLA Modules:
  0.0 67.4 jit_solution(3557383169875863350)
XLA Ops:
  0.6 35.8 %shard_map.166 = (bf16[1,1,3,64,192]{4,3,2,1,0:T(8,128)(2,1)}, bf16[1,1,3,192,512]{4,3,2,1,0:T(8,128)(2,1)}, f32[192,324]{1,0:T(8,128)}) custom-call(s32[1,1,3]{2,1,0:T(1,128)} %valid.1, s32[1,1,2,12]{3,2,1,0:T(2,128)} %lrules.1, s32[1,1,12]{2,1,0:T(1,128)} %lcodes.1, s32[1,1,3,2,3]{4,3,2,1,0:T(2,128)} %bitcast.8, s32[1,3,1,3]{3,2,1,0:T(1,128)} %bitcast.9, ...), custom_call_target="tpu_custom_call" | custom-call | tf_op jit(solution)/shard_map/pallas_call | solution.py:525
  36.5 30.9 %shard_map.167 = (bf16[1,1,3,64,192]{4,3,2,1,0:T(8,128)(2,1)}, bf16[1,1,3,192,512]{4,3,2,1,0:T(8,128)(2,1)}, f32[192,324]{1,0:T(8,128)}) custom-call(bf16[1,1,3,64,192]{4,3,2,1,0:T(8,128)(2,1)} %get-tuple-element.9.a, bf16[1,1,3,192,512]{4,3,2,1,0:T(8,128)(2,1)} %get-tuple-element.10.b, f32[192,324]{1,0:T(8,128)} %get-tuple-element.11.c), custom_call_target="tpu_custom_call" | custom-call | tf_op jit(solution)/shard_map/pallas_call | solution.py:543

commit v4 on v3

--- a/solution.py
+++ b/solution.py
@@ -543,7 +543,7 @@
         out, fgrad, wgrad = pl.pallas_call(
             hand_over,
             out_shape=tuple(jax.ShapeDtypeStruct(a.shape, a.dtype) for a in (out, fgrad, wgrad)),
-            in_specs=[hbm] * 3,
+            in_specs=[vmem] * 3,
             out_specs=(hbm,) * 3,
             scratch_shapes=[pltpu.SemaphoreType.DMA((3,))],
         )(out, fgrad, wgrad)

time: 67.5 us -> 38.8 us (0.57)
  Pallas kernels: 66.8 us -> 38 us
    pallas_call x1, Pallas kernels: 30.9 us -> 2.14 us  [shards(): pl.pallas_call(hand_over, out_shape=tuple((jax.ShapeDtypeStruct(a.shape,...]
where the time goes in v4:
time: 38.8 us; the launch traced here: 38.6 us
  Pallas kernels  38 us (98%)
  between operations  0.64 us (2%)
    pallas_call x1, Pallas kernels, shards(): pl.pallas_call(kernel, out_shape=(jax.ShapeDtypeStruct(cotangent.shape, B...  35.8 us
    pallas_call x1, Pallas kernels, shards(): pl.pallas_call(hand_over, out_shape=tuple((jax.ShapeDtypeStruct(a.shape,...  2.14 us

profile of v4, /device:TPU:0, one launch (start us, length us, event | category | flops | bytes accessed | tf_op | source)
XLA Modules:
  0.0 38.6 jit_solution(2481896456308128841)
XLA Ops:
  0.6 35.8 %shard_map.166 = (bf16[1,1,3,64,192]{4,3,2,1,0:T(8,128)(2,1)}, bf16[1,1,3,192,512]{4,3,2,1,0:T(8,128)(2,1)}, f32[192,324]{1,0:T(8,128)}) custom-call(s32[1,1,3]{2,1,0:T(1,128)} %valid.1, s32[1,1,2,12]{3,2,1,0:T(2,128)} %lrules.1, s32[1,1,12]{2,1,0:T(1,128)} %lcodes.1, s32[1,1,3,2,3]{4,3,2,1,0:T(2,128)} %bitcast.8, s32[1,3,1,3]{3,2,1,0:T(1,128)} %bitcast.9, ...), custom_call_target="tpu_custom_call" | custom-call | tf_op jit(solution)/shard_map/pallas_call | solution.py:525
  36.5 2.1 %shard_map.167 = (bf16[1,1,3,64,192]{4,3,2,1,0:T(8,128)(2,1)}, bf16[1,1,3,192,512]{4,3,2,1,0:T(8,128)(2,1)}, f32[192,324]{1,0:T(8,128)}) custom-call(bf16[1,1,3,64,192]{4,3,2,1,0:T(8,128)(2,1)} %get-tuple-element.9.a, bf16[1,1,3,192,512]{4,3,2,1,0:T(8,128)(2,1)} %get-tuple-element.10.b, f32[192,324]{1,0:T(8,128)} %get-tuple-element.11.c), custom_call_target="tpu_custom_call" | custom-call | tf_op jit(solution)/shard_map/pallas_call | solution.py:543
